TPU v7x, 512 devices: a whole 4x8x8 slice. The times are simulated.
512 devices in a mesh: grp: 16 (over y_lo, z), tp: 8 (over x, core), sp: 4 (over y_hi).
Axes of the slice: x: 4, y: 8 (y_hi: 4, y_lo: 2; y = y_hi * 2 + y_lo), z: 8, core: 2. Of those that a mesh axis runs over, the one named last changes fastest.
Arguments:
- queries: bfloat16 [10240, 8192], P(('grp', 'sp'), 'tp'), may hold values from -6 to 6
- rotated_key_rows: bfloat16 [10240, 1024], P(('grp', 'sp'), 'tp'), may hold values from -6 to 6
- values: bfloat16 [10240, 1024], P(('grp', 'sp'), 'tp'), may hold values from -12 to 12
- packed_prompt_length: int32 [16, 3], P('grp'), may hold values from 1 to 320, 640 in all within a row
- output_projection_weight: bfloat16 [8192, 8192], P('tp', 'sp'), may hold values from -0.0625 to 0.0625
- adapter_down_maps: bfloat16 [64, 64, 8192], P('grp', None, ('tp', 'sp')), may hold values from -0.0625 to 0.0625
- adapter_up_maps: bfloat16 [64, 64, 8192], P('grp', None, ('sp', 'tp')), may hold values from -0.75 to 0.75
- tenant_adapter_slot: int32 [64], replicated, may hold values from 0 to 63, as said below
- tenant_per_block: int32 [16, 5], replicated, may hold values from 0 to 63, as said below
Outputs:
- adapted_layer_output: bfloat16 [10240, 8192], P(('grp', 'tp'), 'sp')
Inputs may be any that keep to these rules, and one draw needn't show every extreme that they name: A permutation: tenant a's adapter is row tenant_adapter_slot[a] of adapter_down_maps and adapter_up_maps, held by grp index tenant_adapter_slot[a] // 4. `tenant_per_block`: the blocks of one group name distinct tenants; at most 1 of a group's tenants have slots held by one grp index, and in every group some grp index holds exactly 1 of them.
All inputs are finite; a program needn't handle non-finite values.
Results may differ from a plain program's by a relative error of at most 0.024.
Values may be sent and summed in bfloat16 or wider, within the bound.
A program may use at most 64 MiB of HBM per device.

v0:
```python
import jax
import jax.numpy as jnp
from jax import lax
from jax.sharding import PartitionSpec as P

HQ = 64
HS = 128
ADAPTER_RANK = 64
BLOCK = 128


adapter_scale = 0.5
big_negative = -1e30


def pack_pages(
    stored_down_maps, stored_up_maps, local_all, owner_all, position, grp_index, slot_cap
):
    chosen = (owner_all[:, :, None] == grp_index) & (
        position[:, :, None] == jnp.arange(slot_cap, dtype=jnp.int32)[None, None, :]
    )
    local_pick = jnp.sum(jnp.where(chosen, local_all[:, :, None], 0), axis=1).reshape(-1)
    filled = jnp.any(chosen, axis=1).reshape(-1)
    send_a = jnp.where(filled[:, None, None], jnp.take(stored_down_maps, local_pick, axis=0), 0)
    send_b = jnp.where(filled[:, None, None], jnp.take(stored_up_maps, local_pick, axis=0), 0)
    return (send_a, send_b)


def on_device(
    queries,
    rotated_key_rows,
    values,
    packed_prompt_length,
    output_projection_weight,
    adapter_down_maps,
    adapter_up_maps,
    tenant_adapter_slot,
    tenant_per_block,
):
    tp_count = lax.axis_size("tp")
    grp_count = lax.axis_size("grp")
    tp_index = lax.axis_index("tp")
    sp_index = lax.axis_index("sp")
    grp_index = lax.axis_index("grp")
    row_count = queries.shape[0]
    heads_dev = HQ // tp_count
    kv_dev = rotated_key_rows.shape[1] // HS
    key_all, value_all = (
        lax.all_gather(rotated_key_rows, "sp", axis=0, tiled=True),
        lax.all_gather(values, "sp", axis=0, tiled=True),
    )
    total_rows = key_all.shape[0]
    lengths = packed_prompt_length[0]
    prompt_ends = jnp.cumsum(lengths)
    prompt_starts = prompt_ends - lengths
    query_pos = sp_index * row_count + jnp.arange(row_count, dtype=jnp.int32)
    key_pos = jnp.arange(total_rows, dtype=jnp.int32)
    inside = (query_pos[:, None] >= prompt_starts[None, :]) & (
        query_pos[:, None] < prompt_ends[None, :]
    )
    prompt_first = jnp.sum(jnp.where(inside, prompt_starts[None, :], 0), axis=1)
    allowed = (key_pos[None, :] <= query_pos[:, None]) & (key_pos[None, :] >= prompt_first[:, None])
    query_heads = queries.reshape(row_count, kv_dev, heads_dev // kv_dev, HS)
    key_heads = key_all.reshape(total_rows, kv_dev, HS)
    scores = jnp.einsum(
        "ikgd,jkd->kgij", query_heads, key_heads, preferred_element_type=jnp.float32
    ) * HS ** (-0.5)
    scores = jnp.where(allowed[None, None], scores, big_negative)
    row_peak = jnp.max(scores, axis=-1, keepdims=True)
    weights = jnp.exp(scores - row_peak)
    attn_probs = (weights / jnp.sum(weights, axis=-1, keepdims=True)).astype(jnp.bfloat16)
    attended = jnp.einsum(
        "kgij,jkd->ikgd",
        attn_probs,
        value_all.reshape(total_rows, kv_dev, HS),
        preferred_element_type=jnp.float32,
    )
    attended = attended.astype(jnp.bfloat16).reshape(row_count, heads_dev * HS)
    block_count = tenant_per_block.shape[1]
    adapter_count = tenant_adapter_slot.shape[0]
    adapter_slot_count = adapter_down_maps.shape[0]
    slot_cap = (block_count + grp_count - 1) // grp_count
    slots_all = jnp.sum(
        jnp.where(
            tenant_per_block[:, :, None]
            == jnp.arange(adapter_count, dtype=jnp.int32)[None, None, :],
            tenant_adapter_slot[None, None, :],
            0,
        ),
        axis=2,
    )
    owner_all = slots_all // adapter_slot_count
    local_all = slots_all % adapter_slot_count
    earlier = jnp.arange(block_count)[None, :] < jnp.arange(block_count)[:, None]
    same_owner = owner_all[:, :, None] == owner_all[:, None, :]
    position = jnp.sum((same_owner & earlier[None]).astype(jnp.int32), axis=2)
    stored_down_maps = lax.all_gather(adapter_down_maps, "sp", axis=2, tiled=True)
    stored_up_maps = lax.all_gather(adapter_up_maps, "tp", axis=2, tiled=True)
    send_a, send_b = pack_pages(
        stored_down_maps, stored_up_maps, local_all, owner_all, position, grp_index, slot_cap
    )
    recv_a, recv_b = (
        lax.all_to_all(send_a, "grp", split_axis=0, concat_axis=0, tiled=True),
        lax.all_to_all(send_b, "grp", split_axis=0, concat_axis=0, tiled=True),
    )
    my_owner = lax.dynamic_index_in_dim(owner_all, grp_index, 0, keepdims=False)
    my_position = lax.dynamic_index_in_dim(position, grp_index, 0, keepdims=False)
    source_index = my_owner * slot_cap + my_position
    gathered = lax.all_gather(attended, "sp", axis=0, tiled=True)
    base_terms = jnp.dot(gathered, output_projection_weight, preferred_element_type=jnp.float32)
    picked_down_map = jnp.take(recv_a, source_index, axis=0)
    input_blocks = gathered.reshape(block_count, BLOCK, gathered.shape[1])
    rank_terms = jnp.einsum(
        "typ,tdp->tyd", input_blocks, picked_down_map, preferred_element_type=jnp.float32
    ).reshape(gathered.shape[0], ADAPTER_RANK)
    base_projection_sum, rank_sum = (
        lax.psum_scatter(
            base_terms.astype(jnp.bfloat16), "tp", scatter_dimension=0, tiled=True
        ).astype(jnp.float32),
        lax.psum_scatter(
            rank_terms.astype(jnp.bfloat16), "tp", scatter_dimension=0, tiled=True
        ).astype(jnp.float32),
    )
    reduced_rank_rows = rank_sum.astype(jnp.bfloat16)
    rows_tp = base_projection_sum.shape[0]
    start_row = tp_index * rows_tp
    cand_count = min(block_count, (rows_tp + BLOCK - 1) // BLOCK + 1)
    first_block = start_row // BLOCK
    candidates = first_block + jnp.arange(cand_count, dtype=jnp.int32)
    page_index = jnp.take(source_index, jnp.minimum(candidates, block_count - 1))
    page_row_list = jnp.take(recv_b, page_index, axis=0)
    adapter_term_list = jnp.einsum(
        "jp,epq->ejq", reduced_rank_rows, page_row_list, preferred_element_type=jnp.float32
    )
    row_block = (start_row + jnp.arange(rows_tp, dtype=jnp.int32)) // BLOCK
    selected_rows = row_block[None, :] == candidates[:, None]
    adapter_delta = jnp.sum(jnp.where(selected_rows[:, :, None], adapter_term_list, 0.0), axis=0)
    return (base_projection_sum + adapter_scale * adapter_delta).astype(jnp.bfloat16)


def solution(mesh):
    return jax.shard_map(
        on_device,
        mesh=mesh,
        in_specs=(
            P(("grp", "sp"), "tp"),
            P(("grp", "sp"), "tp"),
            P(("grp", "sp"), "tp"),
            P("grp", None),
            P("tp", "sp"),
            P("grp", None, ("tp", "sp")),
            P("grp", None, ("sp", "tp")),
            P(),
            P(),
        ),
        out_specs=P(("grp", "tp"), "sp"),
        check_vma=False,
    )
```

profile of v0, /device:TPU:7, one launch (start us, length us, event | category | flops | bytes accessed | tf_op | source)
XLA Modules:
  0.0 239.9 jit_solution(15663059870561822104)
XLA Ops:
  6.5 1.0 select_reduce_fusion
  7.7 15.4 %all_gather.19 = bf16[4,64,1024]{2,1,0:T(8,128)(2,1)S(1)} all-gather(bf16[4,64,256]{2,1,0:T(8,128)(2,1)} %param.14), channel_id=1, replica_groups=mesh['grp'=16,'tp'=8,'sp'=4] {'sp'}, dimensions={2}, use_global_device_ids=true | all-gather | bytes 655360 | tf_op jit(solution)/shard_map/all_gather | solution.py:97
  23.1 0.7 gather_fusion.3
  23.9 1.7 select_select_fusion.1
  25.5 11.2 %all-to-all-start.1 = ((bf16[16,64,1024]{2,1,0:T(8,128)(2,1)}), bf16[16,64,1024]{2,1,0:T(8,128)(2,1)S(1)}, u32[]{:S(2)}, u32[]{:S(2)}) async-start(bf16[16,64,1024]{2,1,0:T(8,128)(2,1)} %select_select_fusion.1), calls=%async_computation.2 | async-start | bytes 4194304 | tf_op jit(solution)/shard_map/all_to_all | solution.py:103
  36.8 0.7 all-gather.5.cloned.1.call-update
  37.5 34.1 %all_gather.15 = bf16[640,128]{1,0:T(8,128)(2,1)S(1)} all-gather(bf16[160,128]{1,0:T(8,128)(2,1)S(1)} %copy-done.1), channel_id=1, replica_groups=mesh['grp'=16,'tp'=8,'sp'=4] {'sp'}, dimensions={0}, use_global_device_ids=true | all-gather | bytes 204800 | tf_op jit(solution)/shard_map/all_gather | solution.py:49
  71.7 11.9 %all_gather.16 = bf16[640,128]{1,0:T(8,128)(2,1)S(1)} all-gather(bf16[160,128]{1,0:T(8,128)(2,1)S(1)} %copy-done.2), channel_id=1, replica_groups=mesh['grp'=16,'tp'=8,'sp'=4] {'sp'}, dimensions={0}, use_global_device_ids=true | all-gather | bytes 204800 | tf_op jit(solution)/shard_map/all_gather | solution.py:50
  84.0 1.0 fusion.1
  85.0 1.1 fusion
  86.1 1.3 fusion.8
  87.6 0.8 copy.39
  88.4 4.0 %gather_fusion.1 = bf16[16,64,2048]{2,1,0:T(8,128)(2,1)} fusion(bf16[4,64,2048]{2,1,0:T(8,128)(2,1)} %all-gather.5.cloned.1.call-done, s32[1024]{0:T(1024)S(1)} %pad_clamp_fusion.3), kind=kCustom, calls=%fused_computation.1 | custom fusion | bytes 8388672 | tf_op jit(solution)/shard_map/jit(_take)/gather | solution.py:25
  92.5 4.7 %select_select_fusion = bf16[16,64,2048]{2,1,0:T(8,128)(2,1)} fusion(bf16[16,64,2048]{2,1,0:T(8,128)(2,1)} %gather_fusion.1, pred[16]{0:T(512)(128)(4,1)S(1)} %compare_and_fusion.2, pred[16]{0:T(512)(128)(4,1)S(1)} %get-tuple-element.5), kind=kLoop, calls=%fused_computation.5 | loop fusion | flops 4194304 | bytes 8388640 | tf_op jit(solution)/shard_map/jit(_where)/select_n | solution.py:25
  97.1 14.5 %all-to-all-start = ((bf16[16,64,2048]{2,1,0:T(8,128)(2,1)}), bf16[16,64,2048]{2,1,0:T(8,128)(2,1)}, u32[]{:S(2)}, u32[]{:S(2)}) async-start(bf16[16,64,2048]{2,1,0:T(8,128)(2,1)} %select_select_fusion), calls=%async_computation.1 | async-start | bytes 8388608 | tf_op jit(solution)/shard_map/all_to_all | solution.py:104
  112.5 40.1 %all-gather.3.cloned.1.call-done = bf16[640,1024]{1,0:T(8,128)(2,1)} async-done(((bf16[160,1024]{1,0:T(8,128)(2,1)}), bf16[640,1024]{1,0:T(8,128)(2,1)}) %all-gather.3.cloned.1.call-update) | async-done | bytes 1310736 | tf_op jit(solution)/shard_map/all_gather | solution.py:109
  152.6 1.9 convolution_convert_fusion.1
  154.5 0.8 copy.28
  155.4 7.0 %convolution_convert_fusion = bf16[640,2048]{1,0:T(8,128)(2,1)} fusion(bf16[640,1024]{1,0:T(8,128)(2,1)} %all-gather.3.cloned.1.call-done, bf16[1024,2048]{1,0:T(8,128)(2,1)} %param.13), kind=kOutput, calls=%fused_computation.9 | convolution fusion | flops 2685665280 | bytes 8126464 | tf_op jit(solution)/shard_map/dot_general | solution.py:110
  163.3 44.4 %all-to-all-done = bf16[16,64,2048]{2,1,0:T(8,128)(2,1)} async-done(((bf16[16,64,2048]{2,1,0:T(8,128)(2,1)}), bf16[16,64,2048]{2,1,0:T(8,128)(2,1)}, u32[]{:S(2)}, u32[]{:S(2)}) %all-to-all-start) | async-done | bytes 4194336 | tf_op jit(solution)/shard_map/all_to_all | solution.py:104
  207.7 2.8 %gather_fusion.2 = bf16[2,64,2048]{2,1,0:T(8,128)(2,1)S(1)} fusion(bf16[16,64,2048]{2,1,0:T(8,128)(2,1)} %all-to-all-done, s32[1024]{0:T(1024)S(1)} %pad_clamp_fusion), kind=kCustom, calls=%fused_computation.2 | custom fusion | bytes 1048584 | tf_op jit(solution)/shard_map/jit(_take)/gather | solution.py:131
  210.5 1.2 fusion.4
  211.7 20.0 %reduce-scatter.5.cloned.1.call-done = bf16[80,2048]{1,0:T(8,128)(2,1)} async-done(((bf16[640,2048]{1,0:T(8,128)(2,1)}), bf16[80,2048]{1,0:T(8,128)(2,1)}) %reduce-scatter.5.cloned.1.call-update) | async-done | bytes 327696 | tf_op jit(solution)/shard_map/reduce_scatter | solution.py:117
  231.6 1.8 fusion.11
  (46 shorter events, 2.6 us)
Async XLA Ops:
  6.5 77.5 %copy-start = (bf16[160,1024]{1,0:T(8,128)(2,1)S(1)}, bf16[160,1024]{1,0:T(8,128)(2,1)}, u32[]{:S(2)}) copy-start(bf16[160,1024]{1,0:T(8,128)(2,1)} %param.9) | copy-start | bytes 983044
  23.8 13.7 %copy-start.1 = (bf16[160,128]{1,0:T(8,128)(2,1)S(1)}, bf16[160,128]{1,0:T(8,128)(2,1)}, u32[]{:S(2)}) copy-start(bf16[160,128]{1,0:T(8,128)(2,1)} %param.10) | copy-start | bytes 122884
  25.5 46.2 %copy-start.2 = (bf16[160,128]{1,0:T(8,128)(2,1)S(1)}, bf16[160,128]{1,0:T(8,128)(2,1)}, u32[]{:S(2)}) copy-start(bf16[160,128]{1,0:T(8,128)(2,1)} %param.11) | copy-start | bytes 122884
  25.5 58.0 %copy-start.3 = (s32[1,3]{1,0:T(1,128)S(1)}, s32[1,3]{1,0:T(1,128)}, u32[]{:S(2)}) copy-start(s32[1,3]{1,0:T(1,128)} %param.12) | copy-start | bytes 40
  25.5 71.6 %all-to-all-start.1 = ((bf16[16,64,1024]{2,1,0:T(8,128)(2,1)}), bf16[16,64,1024]{2,1,0:T(8,128)(2,1)S(1)}, u32[]{:S(2)}, u32[]{:S(2)}) async-start(bf16[16,64,1024]{2,1,0:T(8,128)(2,1)} %select_select_fusion.1), calls=%async_computation.2 | async-start | bytes 4194304 | tf_op jit(solution)/shard_map/all_to_all | solution.py:103
  36.7 51.7 %all-gather.5.cloned.1.call-start = ((), (), s32[]{:S(2)}) async-start(), calls=%async_computation.6 | async-start | bytes 1179648 | tf_op jit(solution)/shard_map/all_gather | solution.py:98
  37.5 115.1 %all-gather.3.cloned.1.call-start = ((), (), s32[]{:S(2)}) async-start(), calls=%async_computation.4 | async-start | bytes 1638400 | tf_op jit(solution)/shard_map/all_gather | solution.py:109
  97.1 110.5 %all-to-all-start = ((bf16[16,64,2048]{2,1,0:T(8,128)(2,1)}), bf16[16,64,2048]{2,1,0:T(8,128)(2,1)}, u32[]{:S(2)}, u32[]{:S(2)}) async-start(bf16[16,64,2048]{2,1,0:T(8,128)(2,1)} %select_select_fusion), calls=%async_computation.1 | async-start | bytes 8388608 | tf_op jit(solution)/shard_map/all_to_all | solution.py:104
  111.6 98.9 %reduce-scatter.7.cloned.1.call-start = ((), (), s32[]{:S(2)}) async-start(), calls=%async_computation.7 | async-start | bytes 184320
  155.4 76.3 %reduce-scatter.5.cloned.1.call-start = ((), (), s32[]{:S(2)}) async-start(), calls=%async_computation.5 | async-start | bytes 2949120 | tf_op jit(solution)/shard_map/reduce_scatter | solution.py:117
Sparse Core Ops, SparseCore 0:
  39.7 31.4 all-gather.4
  88.5 64.0 all-gather.2
  155.5 33.4 reduce-scatter.6
  192.0 39.6 reduce-scatter.4
where the time goes:
time: 241 us; the launch traced here: 240 us
  waiting for transfers between devices  105 us (44%)
  blocking collectives  61.4 us (25%)
  starting transfers between devices  25.9 us (11%)
  between operations  13.4 us (6%)
  matrix products  12.5 us (5%)
  other arithmetic  11.2 us (5%)
  local copies, waits for them, and re-layouts  10.4 us (4%)
    all_to_all x1, waiting for transfers between devices, on_device(): lax.all_to_all(send_b, 'grp', split_axis=0, concat_axis=0, tiled=True)  44.4 us
    all_gather x1, waiting for transfers between devices, on_device(): gathered = lax.all_gather(attended, 'sp', axis=0, tiled=True)  40.1 us
    all_gather x1, blocking collectives, on_device(): lax.all_gather(rotated_key_rows, 'sp', axis=0, tiled=True)  34.1 us
    reduce_scatter x1, waiting for transfers between devices, on_device(): lax.psum_scatter(base_terms.astype(jnp.bfloat16), 'tp', scatter_dimension...  20 us
    all_gather x1, blocking collectives, on_device(): lax.all_gather(adapter_down_maps, 'sp', axis=2, tiled=True)  15.4 us
    all_to_all x1, starting transfers between devices, on_device(): lax.all_to_all(send_b, 'grp', split_axis=0, concat_axis=0, tiled=True)  14.5 us
    all_gather x1, blocking collectives, on_device(): lax.all_gather(values, 'sp', axis=0, tiled=True)  11.9 us
    all_to_all x1, starting transfers between devices, on_device(): lax.all_to_all(send_a, 'grp', split_axis=0, concat_axis=0, tiled=True)  11.2 us
  transfers between devices with their start and end apart: 6, of which 3 were waited for; matrix products, arithmetic and copies ran while one was open for 12% of the time, Pallas kernels for 0%

commit v1 on v0

v1 whole, which is shorter than its diff:
```python
import functools

import jax
import jax.numpy as jnp
from jax import lax
from jax.experimental import pallas as pl
from jax.experimental.pallas import tpu as pltpu
from jax.sharding import PartitionSpec as P

HS = 128
RANK = 64
BLOCK = 128
BLOCKS = 5
NSP = 4
NTP = 8
NCHIP = 4
NZ = 8
SLOTS = 4
HEADS = 8
ROWS = 160
HALF = 80
FEAT = 1024
COLS = 2048
SLICE = 256
PARTS = 2
PCOLS = COLS // PARTS
TILE = 256

adapter_scale = 0.5
big_negative = -1e30
MESH = pl.DeviceIdType.MESH
F32 = jnp.float32
BF16 = jnp.bfloat16


def copy_to(src, dst, ssem, rsem, **axis):
    return pltpu.make_async_remote_copy(
        src_ref=src, dst_ref=dst, send_sem=ssem, recv_sem=rsem, device_id=axis, device_id_type=MESH
    )


def kernel(
    tas, tpb, plen, q_hbm, k_hbm, v_hbm, w_hbm, dn_hbm, up_hbm, out_ref,
    qv, kv, vv, wv, dnv, upv, att, keep, sibs, sibr, xs, xr, fin,
    zs, zr0, zr1, cross, crossr, down, up2own, up2, lsibs, lkeep, lsibr, lxs, lxr, lrs, lrr,
    lsem, kvs, kvr, atts, attr, zss, zrs, crs, crr, ups, upr,
    sbs, sbr, xss, xrs, lbs, lbr, lxss, lxrs, lys, lyr,
):
    sp = lax.axis_index("sp")
    tp = lax.axis_index("tp")
    grp = lax.axis_index("grp")
    chip = tp // 2
    core = tp % 2
    sib = tp + 1 - 2 * core
    y_lo = grp // NZ
    z = grp % NZ
    other = (1 - y_lo) * NZ + z
    zr = (zr0, zr1)
    right = (sp + 1) % NSP
    left = (sp + NSP - 1) % NSP

    loads = [
        pltpu.make_async_copy(q_hbm, qv, lsem.at[0]),
        pltpu.make_async_copy(k_hbm, kv.at[2], lsem.at[1]),
        pltpu.make_async_copy(v_hbm, vv.at[2], lsem.at[2]),
        pltpu.make_async_copy(dn_hbm, dnv, lsem.at[3]),
        pltpu.make_async_copy(up_hbm, upv, lsem.at[4]),
        pltpu.make_async_copy(w_hbm, wv, lsem.at[5]),
    ]
    barrier = pltpu.get_barrier_semaphore()
    for i in range(1, NSP):
        pl.semaphore_signal(barrier, inc=1, device_id={"sp": (sp + i) % NSP}, device_id_type=MESH)
    for i in range(1, NTP):
        pl.semaphore_signal(barrier, inc=1, device_id={"tp": (tp + i) % NTP}, device_id_type=MESH)
    for i in range(1, NZ):
        pl.semaphore_signal(barrier, inc=1, device_id={"grp": y_lo * NZ + (z + i) % NZ}, device_id_type=MESH)
    pl.semaphore_signal(barrier, inc=1, device_id={"grp": other}, device_id_type=MESH)
    for c in loads:
        c.start()
    pl.semaphore_wait(barrier, (NSP - 1) + (NTP - 1) + (NZ - 1) + 1)

    def kv_copies(i):
        to = (sp + i) % NSP
        return [
            copy_to(k_hbm, kv.at[2 - i], kvs.at[0, i - 1], kvr.at[0, i - 1], sp=to),
            copy_to(v_hbm, vv.at[2 - i], kvs.at[1, i - 1], kvr.at[1, i - 1], sp=to),
        ]

    for i in (1, 2):
        @pl.when(sp + i < NSP)
        def _(i=i):
            for c in kv_copies(i):
                c.start()

    loads[3].wait()
    loads[4].wait()

    def slot_of(g, b):
        return tas[tpb[g, b]]

    def pack(t, carry):
        g = t
        pick = jnp.int32(0)
        for b in range(BLOCKS):
            slot = slot_of(g, b)
            pick = pick + jnp.where(slot // SLOTS == grp, slot % SLOTS, 0)
        zs[0, g % NZ, g // NZ] = dnv[pick]
        zs[1, g % NZ, g // NZ] = upv[pick]
        return carry

    lax.fori_loop(0, 2 * NZ, pack, 0)

    def z_copy(m, i):
        to = (z + i) % NZ
        return copy_to(zs.at[m, to], zr[m].at[z], zss.at[m, i - 1], zrs.at[m, i - 1], grp=y_lo * NZ + to)

    for m in range(2):
        for i in range(1, NZ):
            z_copy(m, i).start()
        for j in range(2):
            zr[m][z, j] = zs[m, z, j]

    for c in loads[:3]:
        c.wait()
    for i in (1, 2):
        @pl.when(sp >= i)
        def _(i=i):
            for c in kv_copies(i):
                c.wait_recv()

        @pl.when(sp < i)
        def _(i=i):
            kv[2 - i] = jnp.zeros((ROWS, HS), BF16)
            vv[2 - i] = jnp.zeros((ROWS, HS), BF16)

    end0 = plen[0, 0]
    end1 = end0 + plen[0, 1]
    keys = kv[...].reshape(3 * ROWS, HS)
    vals = vv[...].reshape(3 * ROWS, HS)

    def att_copy(h, to_right):
        k = 1 if (h == 0) == to_right else 3
        slot = 0 if k == 1 else 1
        dst_row = h
        side = 0 if to_right else 1
        return copy_to(
            att.at[0, h], att.at[k, dst_row], atts.at[side, slot], attr.at[side, slot],
            sp=right if to_right else left,
        )

    for h in range(2):
        qpos = sp * ROWS + h * HALF + lax.broadcasted_iota(jnp.int32, (HALF, 3 * ROWS), 0)
        kpos = (sp - 2) * ROWS + lax.broadcasted_iota(jnp.int32, (HALF, 3 * ROWS), 1)
        first = jnp.where(qpos >= end1, end1, jnp.where(qpos >= end0, end0, 0))
        allowed = (kpos <= qpos) & (kpos >= first)
        for n in range(HEADS):
            qh = qv[h * HALF:(h + 1) * HALF, n * HS:(n + 1) * HS]
            s = lax.dot_general(qh, keys, (((1,), (1,)), ((), ())), preferred_element_type=F32)
            s = jnp.where(allowed, s * HS ** -0.5, big_negative)
            p = jnp.exp(s - jnp.max(s, axis=1, keepdims=True))
            total = jnp.sum(p, axis=1, keepdims=True)
            o = jnp.dot(p.astype(BF16), vals, preferred_element_type=F32)
            att[0, h, :, n * HS:(n + 1) * HS] = (o / total).astype(BF16)
        if h == 0:
            att_copy(0, True).start()
        else:
            att_copy(1, False).start()
            att_copy(1, True).start()
            att_copy(0, False).start()
    loads[5].wait()

    relays = [
        copy_to(att.at[1, 0], att.at[2, 0], atts.at[0, 2], attr.at[0, 2], sp=right),
        copy_to(att.at[1, 1], att.at[2, 1], atts.at[1, 2], attr.at[1, 2], sp=left),
    ]

    shift = 2 * core - 1
    keep_block = [sp, (sp + NSP + shift) % NSP, (sp + 2) % NSP, (sp + NSP - shift) % NSP]

    def sib_copy(k, part):
        cols = pl.ds(part * PCOLS, PCOLS)
        return copy_to(sibs.at[k, :, cols], sibr.at[k, :, cols], sbs.at[k, part], sbr.at[k, part], tp=sib)

    def product(k):
        rows = att.at[k]
        for part in range(PARTS):
            def tile(n, carry, part=part):
                cols = pl.ds(pl.multiple_of(part * PCOLS + n * TILE, TILE), TILE)
                v = jnp.dot(
                    rows[...].reshape(ROWS, FEAT), wv[:, cols], preferred_element_type=F32
                )
                keep[k, :, cols] = jnp.where(core == 0, v[:HALF], v[HALF:])
                sibs[k, :, cols] = jnp.where(core == 0, v[HALF:], v[:HALF]).astype(BF16)
                return carry

            lax.fori_loop(0, PCOLS // TILE, tile, 0)
            sib_copy(k, part).start()

    def x_copy(k, part):
        cols = pl.ds(part * PCOLS, PCOLS)
        rel = (chip + NCHIP - keep_block[k] + NCHIP - 1) % NCHIP
        return copy_to(
            xs.at[k, :, cols], xr.at[rel, :, cols], xss.at[k, part], xrs.at[rel, part],
            tp=2 * keep_block[k] + core,
        )

    def x_phase(k):
        for part in range(PARTS):
            cols = pl.ds(part * PCOLS, PCOLS)
            sib_copy(k, part).wait_recv()
            total = keep[k, :, cols] + sibr[k, :, cols].astype(F32)

            @pl.when(keep_block[k] == chip)
            def _():
                fin[:, cols] = total

            @pl.when(keep_block[k] != chip)
            def _():
                xs[k, :, cols] = total.astype(BF16)
                x_copy(k, part).start()

    product(0)

    for side in range(2):
        if side == 0:
            att_copy(0, True).wait_recv()
        else:
            att_copy(1, False).wait_recv()
        relays[side].start()
    x_phase(0)
    product(1)

    def cross_copy(m):
        return copy_to(cross.at[m], crossr.at[m], crs.at[m], crr.at[m], grp=other)

    def cross_send(m):
        for i in range(1, NZ):
            z_copy(m, i).wait_recv()

        def fill(b, carry):
            owner = slot_of(other, b) // SLOTS
            cross[m, b] = zr[m][owner % NZ, 1 - y_lo]
            return carry

        lax.fori_loop(0, BLOCKS, fill, 0)
        cross_copy(m).start()

    def cross_take(m, dst):
        cross_copy(m).wait_recv()

        def fill(b, carry):
            owner = slot_of(grp, b) // SLOTS
            dst[b] = jnp.where(owner // NZ == y_lo, zr[m][owner % NZ, y_lo], crossr[m, b])
            return carry

        lax.fori_loop(0, BLOCKS, fill, 0)

    cross_send(0)
    x_phase(1)
    cross_send(1)

    for side in range(2):
        relays[side].wait_recv()
    product(2)
    cross_take(0, down)
    cross_take(1, up2own)

    def up_copy(i):
        to = (tp + i) % NTP
        return copy_to(up2own.at[pl.ds(to // 2, 2)], up2.at[tp], ups.at[i - 1], upr.at[i - 1], tp=to)

    for i in range(1, NTP):
        up_copy(i).start()
    up2[tp] = up2own[pl.ds(chip, 2)]
    x_phase(2)

    att_copy(0, False).wait_recv()
    att_copy(1, True).wait_recv()

    lane = lax.broadcasted_iota(jnp.int32, (HALF, 2 * RANK), 1)
    row = lax.broadcasted_iota(jnp.int32, (HALF, 2 * RANK), 0)
    features = pl.ds(pl.multiple_of(sp * SLICE, SLICE), SLICE)
    blocks_of = [(sp, sp), (left, right), ((sp + 2) % NSP,) * 2, (right, left)]
    for k in range(4):
        halves = []
        for h in range(2):
            sb = blocks_of[k][h]
            pair = down[pl.ds(sb, 2)].reshape(2 * RANK, SLICE)
            lr = lax.dot_general(
                att[k, h, :, features], pair, (((1,), (1,)), ((), ())), preferred_element_type=F32
            )
            early = (row + h * HALF < BLOCK - (ROWS - BLOCK) * sb).astype(jnp.int32)
            firsts = (lane < RANK).astype(jnp.int32)
            halves.append(jnp.where(early == firsts, lr, 0.0))
        lkeep[k] = jnp.where(core == 0, halves[0], halves[1])
        lsibs[k] = jnp.where(core == 0, halves[1], halves[0]).astype(BF16)
    lsib_copy = copy_to(lsibs, lsibr, lbs, lbr, tp=sib)
    lsib_copy.start()

    product(3)

    def lx_copy(k):
        rel = (chip + NCHIP - keep_block[k] + NCHIP - 1) % NCHIP
        return copy_to(
            lxs.at[k], lxr.at[rel], lxss.at[k], lxrs.at[rel], tp=2 * keep_block[k] + core
        )

    lsib_copy.wait_recv()
    for k in range(4):
        total = lkeep[k] + lsibr[k].astype(F32)

        @pl.when(keep_block[k] == chip)
        def _():
            lrs[...] = total

        @pl.when(keep_block[k] != chip)
        def _():
            lxs[k] = total.astype(BF16)
            lx_copy(k).start()

    x_phase(3)

    for rel in range(NCHIP - 1):
        copy_to(lxs.at[0], lxr.at[rel], lxss.at[0], lxrs.at[rel], tp=sib).wait_recv()
    lrs[...] = lrs[...] + (lxr[0].astype(F32) + lxr[1].astype(F32) + lxr[2].astype(F32))

    def ly_copy(i):
        return copy_to(lrs, lrr.at[i - 1], lys.at[i - 1], lyr.at[i - 1], sp=(sp + i) % NSP)

    for i in range(1, NSP):
        ly_copy(i).start()
    for i in range(1, NTP):
        up_copy(i).wait_recv()
    for i in range(1, NSP):
        ly_copy(i).wait_recv()
    low = (lrs[...] + (lrr[0] + lrr[1] + lrr[2])).astype(BF16)
    for part in range(PARTS):
        cols = pl.ds(part * PCOLS, PCOLS)
        for rel in range(NCHIP - 1):
            copy_to(
                xs.at[0, :, cols], xr.at[rel, :, cols], xss.at[0, part], xrs.at[rel, part], tp=sib
            ).wait_recv()
        for n in range(PCOLS // SLICE):
            j = part * (PCOLS // SLICE) + n
            c = pl.ds(j * SLICE, SLICE)
            delta = jnp.dot(low, up2[j].reshape(2 * RANK, SLICE), preferred_element_type=F32)
            base = fin[:, c] + (
                xr[0, :, c].astype(F32) + xr[1, :, c].astype(F32) + xr[2, :, c].astype(F32)
            )
            out_ref[:, c] = (base + adapter_scale * delta).astype(BF16)

    for i in (1, 2):
        @pl.when(sp + i < NSP)
        def _(i=i):
            for c in kv_copies(i):
                c.wait_send()
    for m in range(2):
        for i in range(1, NZ):
            z_copy(m, i).wait_send()
        cross_copy(m).wait_send()
    for h in range(2):
        for to_right in (True, False):
            att_copy(h, to_right).wait_send()
    for r in relays:
        r.wait_send()
    for i in range(1, NTP):
        up_copy(i).wait_send()
    lsib_copy.wait_send()
    for k in range(4):
        for part in range(PARTS):
            sib_copy(k, part).wait_send()

        @pl.when(keep_block[k] != chip)
        def _():
            lx_copy(k).wait_send()
            for part in range(PARTS):
                x_copy(k, part).wait_send()
    for i in range(1, NSP):
        ly_copy(i).wait_send()


def on_device(q, k, v, plen, w, dn, up, tas, tpb):
    smem = pl.BlockSpec(memory_space=pltpu.SMEM)
    anym = pl.BlockSpec(memory_space=pl.ANY)
    V = pltpu.VMEM
    D = pltpu.SemaphoreType.DMA
    return pl.pallas_call(
        kernel,
        out_shape=jax.ShapeDtypeStruct((HALF, COLS), BF16),
        in_specs=[smem] * 3 + [anym] * 6,
        out_specs=pl.BlockSpec(memory_space=pltpu.VMEM),
        scratch_shapes=[
            V((ROWS, FEAT), BF16),
            V((3, ROWS, HS), BF16),
            V((3, ROWS, HS), BF16),
            V((FEAT, COLS), BF16),
            V((SLOTS, RANK, SLICE), BF16),
            V((SLOTS, RANK, SLICE), BF16),
            V((4, 2, HALF, FEAT), BF16),
            V((4, HALF, COLS), F32),
            V((4, HALF, COLS), BF16),
            V((4, HALF, COLS), BF16),
            V((4, HALF, COLS), BF16),
            V((NCHIP - 1, HALF, COLS), BF16),
            V((HALF, COLS), F32),
            V((2, NZ, 2, RANK, SLICE), BF16),
            V((NZ, 2, RANK, SLICE), BF16),
            V((NZ, 2, RANK, SLICE), BF16),
            V((2, BLOCKS, RANK, SLICE), BF16),
            V((2, BLOCKS, RANK, SLICE), BF16),
            V((BLOCKS, RANK, SLICE), BF16),
            V((BLOCKS, RANK, SLICE), BF16),
            V((NTP, 2, RANK, SLICE), BF16),
            V((4, HALF, 2 * RANK), BF16),
            V((4, HALF, 2 * RANK), F32),
            V((4, HALF, 2 * RANK), BF16),
            V((4, HALF, 2 * RANK), BF16),
            V((NCHIP - 1, HALF, 2 * RANK), BF16),
            V((HALF, 2 * RANK), F32),
            V((NSP - 1, HALF, 2 * RANK), F32),
            D((6,)),
            D((2, 2)), D((2, 2)),
            D((2, 3)), D((2, 3)),
            D((2, NZ - 1)), D((2, NZ - 1)),
            D((2,)), D((2,)),
            D((NTP - 1,)), D((NTP - 1,)),
            D((4, PARTS)), D((4, PARTS)),
            D((4, PARTS)), D((NCHIP - 1, PARTS)),
            D, D,
            D((4,)), D((NCHIP - 1,)),
            D((NSP - 1,)), D((NSP - 1,)),
        ],
        compiler_params=pltpu.CompilerParams(
            collective_id=0, has_side_effects=True, vmem_limit_bytes=56 * 1024 * 1024
        ),
    )(tas, tpb, plen, q, k, v, w, dn, up)


def solution(mesh):
    return jax.shard_map(
        on_device,
        mesh=mesh,
        in_specs=(
            P(("grp", "sp"), "tp"),
            P(("grp", "sp"), "tp"),
            P(("grp", "sp"), "tp"),
            P("grp", None),
            P("tp", "sp"),
            P("grp", None, ("tp", "sp")),
            P("grp", None, ("sp", "tp")),
            P(),
            P(),
        ),
        out_specs=P(("grp", "tp"), "sp"),
        check_vma=False,
    )
```

time: 241 us -> 91.3 us (0.38)
  the two profiles are of different devices: /device:TPU:7 before, /device:TPU:64 now
where the time goes in v1:
time: 91.3 us; the launch traced here: 91.1 us
  Pallas kernels  88 us (96%)
  local copies, waits for them, and re-layouts  3.08 us (3%)
    pallas_call x1, Pallas kernels, on_device(): pl.pallas_call(kernel, out_shape=jax.ShapeDtypeStruct((HALF, COLS), BF16)...  88 us
    unnamed x2, local copies, waits for them, and re-layouts  3.08 us

profile of v1, /device:TPU:64, one launch (start us, length us, event | category | flops | bytes accessed | tf_op | source)
XLA Modules:
  0.0 91.1 jit_solution(13926071216075127069)
XLA Ops:
  0.0 1.4 %copy.10.tpb = s32[16,5]{1,0:T(8,128)} copy(s32[16,5]{0,1:T(8,128)} %param.17) | data formatting | bytes 640 | tf_op args[8]
  1.4 88.0 %shard_map.91 = bf16[80,2048]{1,0:T(8,128)(2,1)} custom-call(s32[64]{0:T(128)} %tas.1, s32[16,5]{1,0:T(8,128)} %copy.10.tpb, s32[1,3]{1,0:T(1,128)} %plen.1, bf16[160,1024]{1,0:T(8,128)(2,1)} %q_hbm.1, bf16[160,128]{1,0:T(8,128)(2,1)} %k_hbm.1, bf16[160,128]{1,0:T(8,128)(2,1)} %v_hbm.1, bf16[1024,2048]{1,0:T(8,128)(2,1)} %w_hbm.1, ...), custom_call_target="tpu_custom_call" | custom-call | tf_op jit(solution)/shard_map/pallas_call | solution.py:387
  89.4 1.7 %copy.12 = bf16[80,2048]{1,0:T(8,128)(2,1)} copy(bf16[80,2048]{1,0:T(8,128)(2,1)} %shard_map.91) | data formatting | bytes 655360

commit v2 on v1

v2 whole, which is shorter than its diff:
```python
import functools

import jax
import jax.numpy as jnp
from jax import lax
from jax.experimental import pallas as pl
from jax.experimental.pallas import tpu as pltpu
from jax.sharding import PartitionSpec as P

HS = 128
RANK = 64
BLOCK = 128
BLOCKS = 5
NSP = 4
NTP = 8
NCHIP = 4
NZ = 8
SLOTS = 4
HEADS = 8
ROWS = 160
HALF = 80
FEAT = 1024
COLS = 2048
SLICE = 256
PARTS = 4
PCOLS = COLS // PARTS
TILE = 256
STACK = 8
PIECES = ((0, 32), (32, 48))

adapter_scale = 0.5
big_negative = -1e30
MESH = pl.DeviceIdType.MESH
F32 = jnp.float32
BF16 = jnp.bfloat16


def copy_to(src, dst, ssem, rsem, **axis):
    return pltpu.make_async_remote_copy(
        src_ref=src, dst_ref=dst, send_sem=ssem, recv_sem=rsem, device_id=axis, device_id_type=MESH
    )


def kernel(
    tas, tpb, plen, q_hbm, k_hbm, v_hbm, w_hbm, dn_hbm, up_hbm, out_ref,
    qv, kv, vv, wv, dnv, upv, probs, att, keep, sibs, sibr, xs, xr, fin,
    zs, zr0, zr1, cross, crossr, down, up2own, up2, lxs, lxr, lrs, lrr,
    lsem, kvs, kvr, atts, attr, zss, zrs, crs, crr, ups, upr,
    sbs, sbr, xss, xrs, lxss, lxrs, lys, lyr,
):
    sp = lax.axis_index("sp")
    tp = lax.axis_index("tp")
    grp = lax.axis_index("grp")
    chip = tp // 2
    core = tp % 2
    sib = tp + 1 - 2 * core
    y_lo = grp // NZ
    z = grp % NZ
    other = (1 - y_lo) * NZ + z
    zr = (zr0, zr1)
    right = (sp + 1) % NSP
    left = (sp + NSP - 1) % NSP

    loads = [
        pltpu.make_async_copy(k_hbm, kv.at[2], lsem.at[0]),
        pltpu.make_async_copy(q_hbm, qv, lsem.at[1]),
        pltpu.make_async_copy(v_hbm, vv.at[2], lsem.at[2]),
        pltpu.make_async_copy(dn_hbm, dnv, lsem.at[3]),
        pltpu.make_async_copy(up_hbm, upv, lsem.at[4]),
        pltpu.make_async_copy(w_hbm, wv, lsem.at[5]),
    ]
    barrier = pltpu.get_barrier_semaphore()
    for i in range(1, NSP):
        pl.semaphore_signal(barrier, inc=1, device_id={"sp": (sp + i) % NSP}, device_id_type=MESH)
    for i in range(1, NTP):
        pl.semaphore_signal(barrier, inc=1, device_id={"tp": (tp + i) % NTP}, device_id_type=MESH)
    for i in range(1, NZ):
        pl.semaphore_signal(barrier, inc=1, device_id={"grp": y_lo * NZ + (z + i) % NZ}, device_id_type=MESH)
    pl.semaphore_signal(barrier, inc=1, device_id={"grp": other}, device_id_type=MESH)
    for c in loads:
        c.start()
    pl.semaphore_wait(barrier, (NSP - 1) + (NTP - 1) + (NZ - 1) + 1)

    def kv_copy(m, i):
        return copy_to(
            (k_hbm, v_hbm)[m], (kv, vv)[m].at[2 - i], kvs.at[m, i - 1], kvr.at[m, i - 1],
            sp=(sp + i) % NSP,
        )

    for m in range(2):
        for i in (1, 2):
            @pl.when(sp + i < NSP)
            def _():
                kv_copy(m, i).start()

    loads[3].wait()
    loads[4].wait()

    def slot_of(g, b):
        return tas[tpb[b, g]]

    def pack(g, carry):
        pick = jnp.int32(0)
        for b in range(BLOCKS):
            slot = slot_of(g, b)
            pick = pick + jnp.where(slot // SLOTS == grp, slot % SLOTS, 0)
        zs[0, g % NZ, g // NZ] = dnv[pick]
        zs[1, g % NZ, g // NZ] = upv[pick]
        return carry

    lax.fori_loop(0, 2 * NZ, pack, 0)

    def z_copy(m, i):
        to = (z + i) % NZ
        return copy_to(
            zs.at[m, to], zr[m].at[z], zss.at[m, i - 1], zrs.at[m, i - 1], grp=y_lo * NZ + to
        )

    for m in range(2):
        for i in range(1, NZ):
            z_copy(m, i).start()
        for j in range(2):
            zr[m][z, j] = zs[m, z, j]

    def kv_ready(m):
        for i in (1, 2):
            @pl.when(sp >= i)
            def _():
                kv_copy(m, i).wait_recv()

            @pl.when(sp < i)
            def _():
                (kv, vv)[m][2 - i] = jnp.zeros((ROWS, HS), BF16)

    loads[0].wait()
    loads[1].wait()
    kv_ready(0)
    end0 = plen[0, 0]
    end1 = end0 + plen[0, 1]
    keys = kv[...].reshape(3 * ROWS, HS)
    for h in range(2):
        qpos = sp * ROWS + h * HALF + lax.broadcasted_iota(jnp.int32, (HALF, 3 * ROWS), 0)
        kpos = (sp - 2) * ROWS + lax.broadcasted_iota(jnp.int32, (HALF, 3 * ROWS), 1)
        first = jnp.where(qpos >= end1, end1, jnp.where(qpos >= end0, end0, 0))
        allowed = (kpos <= qpos) & (kpos >= first)
        for n in range(0, HEADS, STACK):
            qh = jnp.concatenate(
                [qv[h * HALF:(h + 1) * HALF, m * HS:(m + 1) * HS] for m in range(n, n + STACK)], axis=0
            )
            s = lax.dot_general(qh, keys, (((1,), (1,)), ((), ())), preferred_element_type=F32)
            s = jnp.where(
                allowed[None], s.reshape(STACK, HALF, 3 * ROWS) * HS ** -0.5, big_negative
            )
            p = jnp.exp(s - jnp.max(s, axis=2, keepdims=True))
            probs[h, n * HALF:(n + STACK) * HALF] = p.astype(BF16).reshape(STACK * HALF, 3 * ROWS)
    loads[2].wait()
    kv_ready(1)
    vals = jnp.concatenate(
        [vv[...].reshape(3 * ROWS, HS), jnp.ones((3 * ROWS, HS), BF16)], axis=1
    )

    def first_copy(side):
        return copy_to(
            att.at[0, side], att.at[1, side], atts.at[side, 0], attr.at[side, 0],
            sp=(right, left)[side],
        )

    def later_copy(side, piece):
        rows = pl.ds(*PIECES[piece])
        return copy_to(
            att.at[0, 1 - side, rows], att.at[3, 1 - side, rows],
            atts.at[side, 1 + piece], attr.at[side, 1 + piece],
            sp=(right, left)[side],
        )

    def relay(side):
        return copy_to(
            att.at[1, side], att.at[2, side], atts.at[side, 3], attr.at[side, 3],
            sp=(right, left)[side],
        )

    for h in range(2):
        for n in range(0, HEADS, STACK):
            o = jnp.dot(
                probs[h, n * HALF:(n + STACK) * HALF], vals, preferred_element_type=F32
            )
            o = (o[:, :HS] / o[:, HS:]).astype(BF16)
            for m in range(STACK):
                att[0, h, :, (n + m) * HS:(n + m + 1) * HS] = o[m * HALF:(m + 1) * HALF]
        first_copy(h).start()
    for side in range(2):
        later_copy(side, 0).start()
    loads[5].wait()

    shift = 2 * core - 1
    keep_block = [sp, (sp + NSP + shift) % NSP, (sp + 2) % NSP, (sp + NSP - shift) % NSP]

    def sib_copy(k, part):
        cols = pl.ds(part * PCOLS, PCOLS)
        return copy_to(sibs.at[k, :, cols], sibr.at[k, :, cols], sbs.at[k, part], sbr.at[k, part], tp=sib)

    def product(k):
        for part in range(PARTS):
            for n in range(PCOLS // TILE):
                cols = pl.ds(part * PCOLS + n * TILE, TILE)
                v = jnp.dot(
                    att[k].reshape(ROWS, FEAT), wv[:, cols], preferred_element_type=F32
                )
                keep[k, :, cols] = jnp.where(core == 0, v[:HALF], v[HALF:])
                sibs[k, :, cols] = jnp.where(core == 0, v[HALF:], v[:HALF]).astype(BF16)
            sib_copy(k, part).start()

    def x_copy(k, part):
        cols = pl.ds(part * PCOLS, PCOLS)
        rel = (chip + NCHIP - keep_block[k] + NCHIP - 1) % NCHIP
        return copy_to(
            xs.at[k, :, cols], xr.at[rel, :, cols], xss.at[k, part], xrs.at[rel, part],
            tp=2 * keep_block[k] + core,
        )

    def x_phase(k):
        for part in range(PARTS):
            cols = pl.ds(part * PCOLS, PCOLS)
            sib_copy(k, part).wait_recv()
            total = keep[k, :, cols] + sibr[k, :, cols].astype(F32)

            @pl.when(keep_block[k] == chip)
            def _():
                fin[:, cols] = total

            @pl.when(keep_block[k] != chip)
            def _():
                xs[k, :, cols] = total.astype(BF16)
                x_copy(k, part).start()

    lane = lax.broadcasted_iota(jnp.int32, (HALF, 2 * RANK), 1)
    row = lax.broadcasted_iota(jnp.int32, (HALF, 2 * RANK), 0)
    features = pl.ds(pl.multiple_of(sp * SLICE, SLICE), SLICE)
    far = (sp + 2) % NSP
    blocks_of = [(sp, sp), (left, right), (far, far), (right, left)]

    def low_copy(k, h):
        to = 2 * blocks_of[k][h] + h
        rel = (tp + NTP - to + NTP - 1) % NTP
        return copy_to(lxs.at[k, h], lxr.at[rel], lxss.at[k, h], lxrs.at[rel], tp=to)

    def low_rank(k):
        for h in range(2):
            sb = blocks_of[k][h]
            pair = down[pl.ds(sb, 2)].reshape(2 * RANK, SLICE)
            lr = lax.dot_general(
                att[k, h, :, features], pair, (((1,), (1,)), ((), ())), preferred_element_type=F32
            )
            early = (row + h * HALF < BLOCK - (ROWS - BLOCK) * sb).astype(jnp.int32)
            firsts = (lane < RANK).astype(jnp.int32)
            lr = jnp.where(early == firsts, lr, 0.0)

            @pl.when(2 * sb + h == tp)
            def _():
                lrs[...] = lr

            @pl.when(2 * sb + h != tp)
            def _():
                lxs[k, h] = lr.astype(BF16)
                low_copy(k, h).start()

    def cross_copy(m):
        return copy_to(cross.at[m], crossr.at[m], crs.at[m], crr.at[m], grp=other)

    def cross_send(m):
        for i in range(1, NZ):
            z_copy(m, i).wait_recv()

        def fill(b, carry):
            owner = slot_of(other, b) // SLOTS
            cross[m, b] = zr[m][owner % NZ, 1 - y_lo]
            return carry

        lax.fori_loop(0, BLOCKS, fill, 0)
        cross_copy(m).start()

    def cross_take(m, dst):
        cross_copy(m).wait_recv()

        def fill(b, carry):
            owner = slot_of(grp, b) // SLOTS
            dst[b] = jnp.where(owner // NZ == y_lo, zr[m][owner % NZ, y_lo], crossr[m, b])
            return carry

        lax.fori_loop(0, BLOCKS, fill, 0)

    def up_copy(i):
        to = (chip + i) % NCHIP
        return copy_to(
            up2own.at[pl.ds(to, 2)], up2.at[tp], ups.at[i - 1], upr.at[i - 1], tp=2 * to + core
        )

    def up_share(i):
        at = 2 * ((chip + NCHIP - i) % NCHIP) + core
        return copy_to(
            up2.at[at], up2.at[at], ups.at[NCHIP - 1 + i], upr.at[NCHIP - 1 + i], tp=sib
        )

    product(0)

    for side in range(2):
        first_copy(side).wait_recv()
        relay(side).start()
    for side in range(2):
        later_copy(side, 1).start()
    x_phase(0)
    product(1)
    cross_send(0)
    x_phase(1)

    for side in range(2):
        relay(side).wait_recv()
    product(2)
    cross_take(0, down)
    for k in range(3):
        low_rank(k)
    x_phase(2)
    cross_send(1)

    for side in range(2):
        for piece in range(2):
            later_copy(side, piece).wait_recv()
    low_rank(3)
    product(3)
    cross_take(1, up2own)
    for i in range(1, NCHIP):
        up_copy(i).start()
    up2[tp] = up2own[pl.ds(chip, 2)]
    up_share(0).start()
    x_phase(3)

    for rel in range(NTP - 1):
        copy_to(lxs.at[0, 0], lxr.at[rel], lxss.at[0, 0], lxrs.at[rel], tp=sib).wait_recv()
    low = lrs[...]
    for rel in range(NTP - 1):
        low = low + lxr[rel].astype(F32)
    lrs[...] = low

    def ly_copy(i):
        return copy_to(lrs, lrr.at[i - 1], lys.at[i - 1], lyr.at[i - 1], sp=(sp + i) % NSP)

    for i in range(1, NSP):
        ly_copy(i).start()
    for i in range(1, NCHIP):
        up_copy(i).wait_recv()
        up_share(i).start()
    for i in range(1, NSP):
        ly_copy(i).wait_recv()
    low = (lrs[...] + (lrr[0] + lrr[1] + lrr[2])).astype(BF16)
    for i in range(NCHIP):
        up_share(i).wait_recv()
    for part in range(PARTS):
        cols = pl.ds(part * PCOLS, PCOLS)
        for rel in range(NCHIP - 1):
            copy_to(
                xs.at[0, :, cols], xr.at[rel, :, cols], xss.at[0, part], xrs.at[rel, part], tp=sib
            ).wait_recv()
        for n in range(PCOLS // SLICE):
            j = part * (PCOLS // SLICE) + n
            c = pl.ds(j * SLICE, SLICE)
            delta = jnp.dot(low, up2[j].reshape(2 * RANK, SLICE), preferred_element_type=F32)
            base = fin[:, c] + (
                xr[0, :, c].astype(F32) + xr[1, :, c].astype(F32) + xr[2, :, c].astype(F32)
            )
            out_ref[:, c] = (base + adapter_scale * delta).astype(BF16)

    for m in range(2):
        for i in (1, 2):
            @pl.when(sp + i < NSP)
            def _():
                kv_copy(m, i).wait_send()
        for i in range(1, NZ):
            z_copy(m, i).wait_send()
        cross_copy(m).wait_send()
    for side in range(2):
        first_copy(side).wait_send()
        relay(side).wait_send()
        for piece in range(2):
            later_copy(side, piece).wait_send()
    for i in range(1, NCHIP):
        up_copy(i).wait_send()
    for i in range(NCHIP):
        up_share(i).wait_send()
    for k in range(4):
        for part in range(PARTS):
            sib_copy(k, part).wait_send()

        @pl.when(keep_block[k] != chip)
        def _():
            for part in range(PARTS):
                x_copy(k, part).wait_send()

        for h in range(2):
            @pl.when(2 * blocks_of[k][h] + h != tp)
            def _():
                low_copy(k, h).wait_send()
    for i in range(1, NSP):
        ly_copy(i).wait_send()


def on_device(q, k, v, plen, w, dn, up, tas, tpb):
    smem = pl.BlockSpec(memory_space=pltpu.SMEM)
    anym = pl.BlockSpec(memory_space=pl.ANY)
    V = pltpu.VMEM
    D = pltpu.SemaphoreType.DMA
    return pl.pallas_call(
        kernel,
        out_shape=jax.ShapeDtypeStruct((HALF, COLS), BF16),
        in_specs=[smem] * 3 + [anym] * 6,
        out_specs=pl.BlockSpec(memory_space=pltpu.VMEM),
        scratch_shapes=[
            V((ROWS, FEAT), BF16),
            V((3, ROWS, HS), BF16),
            V((3, ROWS, HS), BF16),
            V((FEAT, COLS), BF16),
            V((SLOTS, RANK, SLICE), BF16),
            V((SLOTS, RANK, SLICE), BF16),
            V((2, HEADS * HALF, 3 * ROWS), BF16),
            V((4, 2, HALF, FEAT), BF16),
            V((4, HALF, COLS), F32),
            V((4, HALF, COLS), BF16),
            V((4, HALF, COLS), BF16),
            V((4, HALF, COLS), BF16),
            V((NCHIP - 1, HALF, COLS), BF16),
            V((HALF, COLS), F32),
            V((2, NZ, 2, RANK, SLICE), BF16),
            V((NZ, 2, RANK, SLICE), BF16),
            V((NZ, 2, RANK, SLICE), BF16),
            V((2, BLOCKS, RANK, SLICE), BF16),
            V((2, BLOCKS, RANK, SLICE), BF16),
            V((BLOCKS, RANK, SLICE), BF16),
            V((BLOCKS, RANK, SLICE), BF16),
            V((NTP, 2, RANK, SLICE), BF16),
            V((4, 2, HALF, 2 * RANK), BF16),
            V((NTP - 1, HALF, 2 * RANK), BF16),
            V((HALF, 2 * RANK), F32),
            V((NSP - 1, HALF, 2 * RANK), F32),
            D((6,)),
            D((2, 2)), D((2, 2)),
            D((2, 4)), D((2, 4)),
            D((2, NZ - 1)), D((2, NZ - 1)),
            D((2,)), D((2,)),
            D((2 * NCHIP - 1,)), D((2 * NCHIP - 1,)),
            D((4, PARTS)), D((4, PARTS)),
            D((4, PARTS)), D((NCHIP - 1, PARTS)),
            D((4, 2)), D((NTP - 1,)),
            D((NSP - 1,)), D((NSP - 1,)),
        ],
        compiler_params=pltpu.CompilerParams(
            collective_id=0, has_side_effects=True, vmem_limit_bytes=56 * 1024 * 1024
        ),
    )(tas, tpb.T, plen, q, k, v, w, dn, up)


def solution(mesh):
    return jax.shard_map(
        on_device,
        mesh=mesh,
        in_specs=(
            P(("grp", "sp"), "tp"),
            P(("grp", "sp"), "tp"),
            P(("grp", "sp"), "tp"),
            P("grp", None),
            P("tp", "sp"),
            P("grp", None, ("tp", "sp")),
            P("grp", None, ("sp", "tp")),
            P(),
            P(),
        ),
        out_specs=P(("grp", "tp"), "sp"),
        check_vma=False,
    )
```

time: 91.3 us -> 76.2 us (0.83)
  the two profiles are of different devices: /device:TPU:64 before, /device:TPU:33 now
where the time goes in v2:
time: 76.2 us; the launch traced here: 76 us
  Pallas kernels  74.3 us (98%)
  local copies, waits for them, and re-layouts  1.72 us (2%)
    pallas_call x1, Pallas kernels, on_device(): pl.pallas_call(kernel, out_shape=jax.ShapeDtypeStruct((HALF, COLS), BF16)...  74.3 us
    unnamed x1, local copies, waits for them, and re-layouts  1.72 us

profile of v2, /device:TPU:33, one launch (start us, length us, event | category | flops | bytes accessed | tf_op | source)
XLA Modules:
  0.0 76.0 jit_solution(18105893247800438369)
XLA Ops:
  0.0 74.3 %shard_map.91 = bf16[80,2048]{1,0:T(8,128)(2,1)} custom-call(s32[64]{0:T(128)} %tas.1, s32[5,16]{1,0:T(8,128)} %bitcast.1, s32[1,3]{1,0:T(1,128)} %plen.1, bf16[160,1024]{1,0:T(8,128)(2,1)} %q_hbm.1, bf16[160,128]{1,0:T(8,128)(2,1)} %k_hbm.1, bf16[160,128]{1,0:T(8,128)(2,1)} %v_hbm.1, bf16[1024,2048]{1,0:T(8,128)(2,1)} %w_hbm.1, bf16[4,64,256]{2,1,0:T(8,128)(2,1)} %dn_hbm.1, ...), custom_call_target="tpu_custom_call" | custom-call | tf_op jit(solution)/shard_map/pallas_call | solution.py:411
  74.3 1.7 %copy.11 = bf16[80,2048]{1,0:T(8,128)(2,1)} copy(bf16[80,2048]{1,0:T(8,128)(2,1)} %shard_map.91) | data formatting | bytes 655360

commit v3 on v2

--- a/solution.py
+++ b/solution.py
@@ -43,10 +43,10 @@
 
 def kernel(
     tas, tpb, plen, q_hbm, k_hbm, v_hbm, w_hbm, dn_hbm, up_hbm, out_ref,
-    qv, kv, vv, wv, dnv, upv, probs, att, keep, sibs, sibr, xs, xr, fin,
+    qv, kv, vv, wv, dnv, upv, probs, att, keep, sibs, sibr, xs, xr, hop, fin,
     zs, zr0, zr1, cross, crossr, down, up2own, up2, lxs, lxr, lrs, lrr,
     lsem, kvs, kvr, atts, attr, zss, zrs, crs, crr, ups, upr,
-    sbs, sbr, xss, xrs, lxss, lxrs, lys, lyr,
+    sbs, sbr, xss, xrs, txs, txr, lxss, lxrs, lys, lyr,
 ):
     sp = lax.axis_index("sp")
     tp = lax.axis_index("tp")
@@ -199,16 +199,19 @@
         cols = pl.ds(part * PCOLS, PCOLS)
         return copy_to(sibs.at[k, :, cols], sibr.at[k, :, cols], sbs.at[k, part], sbr.at[k, part], tp=sib)
 
+    def product_part(k, part):
+        for n in range(PCOLS // TILE):
+            cols = pl.ds(part * PCOLS + n * TILE, TILE)
+            v = jnp.dot(
+                att[k].reshape(ROWS, FEAT), wv[:, cols], preferred_element_type=F32
+            )
+            keep[k, :, cols] = jnp.where(core == 0, v[:HALF], v[HALF:])
+            sibs[k, :, cols] = jnp.where(core == 0, v[HALF:], v[:HALF]).astype(BF16)
+        sib_copy(k, part).start()
+
     def product(k):
         for part in range(PARTS):
-            for n in range(PCOLS // TILE):
-                cols = pl.ds(part * PCOLS + n * TILE, TILE)
-                v = jnp.dot(
-                    att[k].reshape(ROWS, FEAT), wv[:, cols], preferred_element_type=F32
-                )
-                keep[k, :, cols] = jnp.where(core == 0, v[:HALF], v[HALF:])
-                sibs[k, :, cols] = jnp.where(core == 0, v[HALF:], v[:HALF]).astype(BF16)
-            sib_copy(k, part).start()
+            product_part(k, part)
 
     def x_copy(k, part):
         cols = pl.ds(part * PCOLS, PCOLS)
@@ -218,25 +221,80 @@
             tp=2 * keep_block[k] + core,
         )
 
+    def x_part(k, part):
+        cols = pl.ds(part * PCOLS, PCOLS)
+        sib_copy(k, part).wait_recv()
+        total = keep[k, :, cols] + sibr[k, :, cols].astype(F32)
+
+        @pl.when(keep_block[k] == chip)
+        def _():
+            fin[:, cols] = total
+
+        @pl.when(keep_block[k] != chip)
+        def _():
+            xs[k, :, cols] = total.astype(BF16)
+            x_copy(k, part).start()
+
     def x_phase(k):
         for part in range(PARTS):
+            x_part(k, part)
+
+    far = (sp + 2) % NSP
+    place = (chip + NCHIP - far) % NCHIP
+
+    def tree_copy(part):
+        cols = pl.ds(part * PCOLS, PCOLS)
+        side = part // (PARTS // 2)
+        to = (far + (1, NCHIP - 1)[side]) % NCHIP
+        return copy_to(
+            xs.at[2, :, cols], hop.at[part % (PARTS // 2)], txs.at[part], txr.at[part % (PARTS // 2)],
+            tp=2 * to + core,
+        )
+
+    def far_phase():
+        k = 2
+        for part in range(PARTS):
             cols = pl.ds(part * PCOLS, PCOLS)
+            side = part // (PARTS // 2)
             sib_copy(k, part).wait_recv()
             total = keep[k, :, cols] + sibr[k, :, cols].astype(F32)
 
-            @pl.when(keep_block[k] == chip)
+            @pl.when(place == 0)
             def _():
                 fin[:, cols] = total
 
-            @pl.when(keep_block[k] != chip)
+            @pl.when(place == 2)
+            def _():
+                xs[k, :, cols] = total.astype(BF16)
+                tree_copy(part).start()
+
+            @pl.when(place == (3, 1)[side])
             def _():
                 xs[k, :, cols] = total.astype(BF16)
                 x_copy(k, part).start()
+
+            @pl.when(place == (1, 3)[side])
+            def _():
+                keep[k, :, cols] = total
+
+        for part in range(PARTS):
+            cols = pl.ds(part * PCOLS, PCOLS)
+            side = part // (PARTS // 2)
+
+            @pl.when(place == (1, 3)[side])
+            def _():
+                tree_copy(part).wait_recv()
+                total = keep[k, :, cols] + hop[part % (PARTS // 2)].astype(F32)
+                xs[k, :, cols] = total.astype(BF16)
+                x_copy(k, part).start()
+
+        @pl.when(place == 0)
+        def _():
+            xr[1] = jnp.zeros((HALF, COLS), BF16)
 
     lane = lax.broadcasted_iota(jnp.int32, (HALF, 2 * RANK), 1)
     row = lax.broadcasted_iota(jnp.int32, (HALF, 2 * RANK), 0)
     features = pl.ds(pl.multiple_of(sp * SLICE, SLICE), SLICE)
-    far = (sp + 2) % NSP
     blocks_of = [(sp, sp), (left, right), (far, far), (right, left)]
 
     def low_copy(k, h):
@@ -319,20 +377,23 @@
     cross_take(0, down)
     for k in range(3):
         low_rank(k)
-    x_phase(2)
-    cross_send(1)
+    far_phase()
 
     for side in range(2):
         for piece in range(2):
             later_copy(side, piece).wait_recv()
+    cross_send(1)
     low_rank(3)
-    product(3)
+    for part in range(PARTS):
+        product_part(3, part)
+        if part > 0:
+            x_part(3, part - 1)
+    x_part(3, PARTS - 1)
     cross_take(1, up2own)
     for i in range(1, NCHIP):
         up_copy(i).start()
     up2[tp] = up2own[pl.ds(chip, 2)]
     up_share(0).start()
-    x_phase(3)
 
     for rel in range(NTP - 1):
         copy_to(lxs.at[0, 0], lxr.at[rel], lxss.at[0, 0], lxrs.at[rel], tp=sib).wait_recv()
@@ -357,9 +418,15 @@
     for part in range(PARTS):
         cols = pl.ds(part * PCOLS, PCOLS)
         for rel in range(NCHIP - 1):
-            copy_to(
+            came = copy_to(
                 xs.at[0, :, cols], xr.at[rel, :, cols], xss.at[0, part], xrs.at[rel, part], tp=sib
-            ).wait_recv()
+            )
+            if rel == 1:
+                @pl.when(place != 0)
+                def _():
+                    came.wait_recv()
+            else:
+                came.wait_recv()
         for n in range(PCOLS // SLICE):
             j = part * (PCOLS // SLICE) + n
             c = pl.ds(j * SLICE, SLICE)
@@ -390,10 +457,21 @@
         for part in range(PARTS):
             sib_copy(k, part).wait_send()
 
-        @pl.when(keep_block[k] != chip)
-        def _():
-            for part in range(PARTS):
-                x_copy(k, part).wait_send()
+        if k == 2:
+            @pl.when(place == 2)
+            def _():
+                for part in range(PARTS):
+                    tree_copy(part).wait_send()
+
+            @pl.when(place % 2 == 1)
+            def _():
+                for part in range(PARTS):
+                    x_copy(k, part).wait_send()
+        else:
+            @pl.when(keep_block[k] != chip)
+            def _():
+                for part in range(PARTS):
+                    x_copy(k, part).wait_send()
 
         for h in range(2):
             @pl.when(2 * blocks_of[k][h] + h != tp)
@@ -427,6 +505,7 @@
             V((4, HALF, COLS), BF16),
             V((4, HALF, COLS), BF16),
             V((NCHIP - 1, HALF, COLS), BF16),
+            V((PARTS // 2, HALF, PCOLS), BF16),
             V((HALF, COLS), F32),
             V((2, NZ, 2, RANK, SLICE), BF16),
             V((NZ, 2, RANK, SLICE), BF16),
@@ -448,6 +527,7 @@
             D((2 * NCHIP - 1,)), D((2 * NCHIP - 1,)),
             D((4, PARTS)), D((4, PARTS)),
             D((4, PARTS)), D((NCHIP - 1, PARTS)),
+            D((PARTS,)), D((PARTS // 2,)),
             D((4, 2)), D((NTP - 1,)),
             D((NSP - 1,)), D((NSP - 1,)),
         ],

time: 76.2 us -> 73.1 us (0.959)
  the two profiles are of different devices: /device:TPU:33 before, /device:TPU:17 now
where the time goes in v3:
time: 73.1 us; the launch traced here: 72.9 us
  Pallas kernels  71.2 us (97%)
  local copies, waits for them, and re-layouts  1.72 us (2%)
    pallas_call x1, Pallas kernels, on_device(): pl.pallas_call(kernel, out_shape=jax.ShapeDtypeStruct((HALF, COLS), BF16)...  71.2 us
    unnamed x1, local copies, waits for them, and re-layouts  1.72 us

profile of v3, /device:TPU:17, one launch (start us, length us, event | category | flops | bytes accessed | tf_op | source)
XLA Modules:
  0.0 72.9 jit_solution(5345523398131711030)
XLA Ops:
  0.0 71.2 %shard_map.91 = bf16[80,2048]{1,0:T(8,128)(2,1)} custom-call(s32[64]{0:T(128)} %tas.1, s32[5,16]{1,0:T(8,128)} %bitcast.1, s32[1,3]{1,0:T(1,128)} %plen.1, bf16[160,1024]{1,0:T(8,128)(2,1)} %q_hbm.1, bf16[160,128]{1,0:T(8,128)(2,1)} %k_hbm.1, bf16[160,128]{1,0:T(8,128)(2,1)} %v_hbm.1, bf16[1024,2048]{1,0:T(8,128)(2,1)} %w_hbm.1, bf16[4,64,256]{2,1,0:T(8,128)(2,1)} %dn_hbm.1, ...), custom_call_target="tpu_custom_call" | custom-call | tf_op jit(solution)/shard_map/pallas_call | solution.py:489
  71.2 1.7 %copy.11 = bf16[80,2048]{1,0:T(8,128)(2,1)} copy(bf16[80,2048]{1,0:T(8,128)(2,1)} %shard_map.91) | data formatting | bytes 655360

commit v4 on v3

--- a/solution.py
+++ b/solution.py
@@ -46,7 +46,7 @@
     qv, kv, vv, wv, dnv, upv, probs, att, keep, sibs, sibr, xs, xr, hop, fin,
     zs, zr0, zr1, cross, crossr, down, up2own, up2, lxs, lxr, lrs, lrr,
     lsem, kvs, kvr, atts, attr, zss, zrs, crs, crr, ups, upr,
-    sbs, sbr, xss, xrs, txs, txr, lxss, lxrs, lys, lyr,
+    sbs, sbr, xss, xrs, txs, txr, lxss, lxrs, lys, lyr, z_in,
 ):
     sp = lax.axis_index("sp")
     tp = lax.axis_index("tp")
@@ -74,12 +74,20 @@
         pl.semaphore_signal(barrier, inc=1, device_id={"sp": (sp + i) % NSP}, device_id_type=MESH)
     for i in range(1, NTP):
         pl.semaphore_signal(barrier, inc=1, device_id={"tp": (tp + i) % NTP}, device_id_type=MESH)
+    pl.semaphore_signal(barrier, inc=1, device_id={"grp": other}, device_id_type=MESH)
     for i in range(1, NZ):
-        pl.semaphore_signal(barrier, inc=1, device_id={"grp": y_lo * NZ + (z + i) % NZ}, device_id_type=MESH)
-    pl.semaphore_signal(barrier, inc=1, device_id={"grp": other}, device_id_type=MESH)
+        @pl.when(z + i < NZ)
+        def _():
+            pl.semaphore_signal(barrier, inc=1, device_id={"grp": grp + i}, device_id_type=MESH)
+
     for c in loads:
         c.start()
-    pl.semaphore_wait(barrier, (NSP - 1) + (NTP - 1) + (NZ - 1) + 1)
+    pl.semaphore_wait(barrier, (NSP - 1) + (NTP - 1) + 1 + z)
+    for i in range(1, NZ):
+        @pl.when(z >= i)
+        def _():
+            pl.semaphore_signal(z_in, inc=1, device_id={"grp": grp - i}, device_id_type=MESH)
+
 
     def kv_copy(m, i):
         return copy_to(
@@ -118,7 +126,10 @@
 
     for m in range(2):
         for i in range(1, NZ):
-            z_copy(m, i).start()
+            @pl.when(z + i >= NZ)
+            def _():
+                z_copy(m, i).start()
+
         for j in range(2):
             zr[m][z, j] = zs[m, z, j]
 
@@ -190,6 +201,17 @@
         first_copy(h).start()
     for side in range(2):
         later_copy(side, 0).start()
+
+    @pl.when(z < NZ - 1)
+    def _():
+        pl.semaphore_wait(z_in, NZ - 1 - z)
+
+    for m in range(2):
+        for i in range(1, NZ):
+            @pl.when(z + i < NZ)
+            def _():
+                z_copy(m, i).start()
+
     loads[5].wait()
 
     shift = 2 * core - 1
@@ -368,27 +390,26 @@
         later_copy(side, 1).start()
     x_phase(0)
     product(1)
-    cross_send(0)
     x_phase(1)
 
     for side in range(2):
         relay(side).wait_recv()
     product(2)
-    cross_take(0, down)
-    for k in range(3):
-        low_rank(k)
     far_phase()
 
     for side in range(2):
         for piece in range(2):
             later_copy(side, piece).wait_recv()
+    cross_send(0)
     cross_send(1)
-    low_rank(3)
     for part in range(PARTS):
         product_part(3, part)
         if part > 0:
             x_part(3, part - 1)
     x_part(3, PARTS - 1)
+    cross_take(0, down)
+    for k in range(4):
+        low_rank(k)
     cross_take(1, up2own)
     for i in range(1, NCHIP):
         up_copy(i).start()
@@ -530,6 +551,7 @@
             D((PARTS,)), D((PARTS // 2,)),
             D((4, 2)), D((NTP - 1,)),
             D((NSP - 1,)), D((NSP - 1,)),
+            pltpu.SemaphoreType.REGULAR,
         ],
         compiler_params=pltpu.CompilerParams(
             collective_id=0, has_side_effects=True, vmem_limit_bytes=56 * 1024 * 1024

time: 73.1 us -> 71.4 us (0.977)
  the two profiles are of different devices: /device:TPU:17 before, /device:TPU:1 now
where the time goes in v4:
time: 71.4 us; the launch traced here: 71.2 us
  Pallas kernels  69.5 us (97%)
  local copies, waits for them, and re-layouts  1.72 us (2%)
    pallas_call x1, Pallas kernels, on_device(): pl.pallas_call(kernel, out_shape=jax.ShapeDtypeStruct((HALF, COLS), BF16)...  69.5 us
    unnamed x1, local copies, waits for them, and re-layouts  1.72 us

profile of v4, /device:TPU:1, one launch (start us, length us, event | category | flops | bytes accessed | tf_op | source)
XLA Modules:
  0.0 71.2 jit_solution(1648934816975474726)
XLA Ops:
  0.0 69.5 %shard_map.91 = bf16[80,2048]{1,0:T(8,128)(2,1)} custom-call(s32[64]{0:T(128)} %tas.1, s32[5,16]{1,0:T(8,128)} %bitcast.1, s32[1,3]{1,0:T(1,128)} %plen.1, bf16[160,1024]{1,0:T(8,128)(2,1)} %q_hbm.1, bf16[160,128]{1,0:T(8,128)(2,1)} %k_hbm.1, bf16[160,128]{1,0:T(8,128)(2,1)} %v_hbm.1, bf16[1024,2048]{1,0:T(8,128)(2,1)} %w_hbm.1, bf16[4,64,256]{2,1,0:T(8,128)(2,1)} %dn_hbm.1, ...), custom_call_target="tpu_custom_call" | custom-call | tf_op jit(solution)/shard_map/pallas_call | solution.py:510
  69.5 1.7 %copy.11 = bf16[80,2048]{1,0:T(8,128)(2,1)} copy(bf16[80,2048]{1,0:T(8,128)(2,1)} %shard_map.91) | data formatting | bytes 655360

commit v5 on v4

--- a/solution.py
+++ b/solution.py
@@ -44,7 +44,7 @@
 def kernel(
     tas, tpb, plen, q_hbm, k_hbm, v_hbm, w_hbm, dn_hbm, up_hbm, out_ref,
     qv, kv, vv, wv, dnv, upv, probs, att, keep, sibs, sibr, xs, xr, hop, fin,
-    zs, zr0, zr1, cross, crossr, down, up2own, up2, lxs, lxr, lrs, lrr,
+    zs, zr0, zr1, cross, crossr, down, up2own, up2, lxs, lxr, lrs, lyx, lrr,
     lsem, kvs, kvr, atts, attr, zss, zrs, crs, crr, ups, upr,
     sbs, sbr, xss, xrs, txs, txr, lxss, lxrs, lys, lyr, z_in,
 ):
@@ -124,12 +124,12 @@
             zs.at[m, to], zr[m].at[z], zss.at[m, i - 1], zrs.at[m, i - 1], grp=y_lo * NZ + to
         )
 
+    for i in range(1, NZ):
+        @pl.when(z + i >= NZ)
+        def _():
+            z_copy(0, i).start()
+
     for m in range(2):
-        for i in range(1, NZ):
-            @pl.when(z + i >= NZ)
-            def _():
-                z_copy(m, i).start()
-
         for j in range(2):
             zr[m][z, j] = zs[m, z, j]
 
@@ -206,11 +206,10 @@
     def _():
         pl.semaphore_wait(z_in, NZ - 1 - z)
 
-    for m in range(2):
-        for i in range(1, NZ):
-            @pl.when(z + i < NZ)
-            def _():
-                z_copy(m, i).start()
+    for i in range(1, NZ):
+        @pl.when(z + i < NZ)
+        def _():
+            z_copy(0, i).start()
 
     loads[5].wait()
 
@@ -389,32 +388,29 @@
     for side in range(2):
         later_copy(side, 1).start()
     x_phase(0)
+    for i in range(1, NZ):
+        z_copy(1, i).start()
     product(1)
     x_phase(1)
+    cross_send(0)
 
     for side in range(2):
         relay(side).wait_recv()
     product(2)
     far_phase()
+    cross_take(0, down)
+    for k in range(3):
+        low_rank(k)
 
     for side in range(2):
         for piece in range(2):
             later_copy(side, piece).wait_recv()
-    cross_send(0)
-    cross_send(1)
+    low_rank(3)
     for part in range(PARTS):
         product_part(3, part)
         if part > 0:
             x_part(3, part - 1)
     x_part(3, PARTS - 1)
-    cross_take(0, down)
-    for k in range(4):
-        low_rank(k)
-    cross_take(1, up2own)
-    for i in range(1, NCHIP):
-        up_copy(i).start()
-    up2[tp] = up2own[pl.ds(chip, 2)]
-    up_share(0).start()
 
     for rel in range(NTP - 1):
         copy_to(lxs.at[0, 0], lxr.at[rel], lxss.at[0, 0], lxrs.at[rel], tp=sib).wait_recv()
@@ -422,18 +418,29 @@
     for rel in range(NTP - 1):
         low = low + lxr[rel].astype(F32)
     lrs[...] = low
+    lyx[...] = low.astype(BF16)
 
     def ly_copy(i):
-        return copy_to(lrs, lrr.at[i - 1], lys.at[i - 1], lyr.at[i - 1], sp=(sp + i) % NSP)
+        return copy_to(lyx, lrr.at[i - 1], lys.at[i - 1], lyr.at[i - 1], sp=(sp + i) % NSP)
 
     for i in range(1, NSP):
         ly_copy(i).start()
+
+    cross_send(1)
+    cross_take(1, up2own)
+    for i in range(1, NCHIP):
+        up_copy(i).start()
+    up2[tp] = up2own[pl.ds(chip, 2)]
+    up_share(0).start()
     for i in range(1, NCHIP):
         up_copy(i).wait_recv()
         up_share(i).start()
     for i in range(1, NSP):
         ly_copy(i).wait_recv()
-    low = (lrs[...] + (lrr[0] + lrr[1] + lrr[2])).astype(BF16)
+    low = lrs[...]
+    for i in range(NSP - 1):
+        low = low + lrr[i].astype(F32)
+    low = low.astype(BF16)
     for i in range(NCHIP):
         up_share(i).wait_recv()
     for part in range(PARTS):
@@ -539,7 +546,8 @@
             V((4, 2, HALF, 2 * RANK), BF16),
             V((NTP - 1, HALF, 2 * RANK), BF16),
             V((HALF, 2 * RANK), F32),
-            V((NSP - 1, HALF, 2 * RANK), F32),
+            V((HALF, 2 * RANK), BF16),
+            V((NSP - 1, HALF, 2 * RANK), BF16),
             D((6,)),
             D((2, 2)), D((2, 2)),
             D((2, 4)), D((2, 4)),

time: 71.4 us -> 73.3 us (1.027)
  the two profiles are of different devices: /device:TPU:1 before, /device:TPU:17 now
where the time goes in v5:
time: 73.3 us; the launch traced here: 73.2 us
  Pallas kernels  71.4 us (97%)
  local copies, waits for them, and re-layouts  1.72 us (2%)
    pallas_call x1, Pallas kernels, on_device(): pl.pallas_call(kernel, out_shape=jax.ShapeDtypeStruct((HALF, COLS), BF16)...  71.4 us
    unnamed x1, local copies, waits for them, and re-layouts  1.72 us

profile of v5, /device:TPU:17, one launch (start us, length us, event | category | flops | bytes accessed | tf_op | source)
XLA Modules:
  0.0 73.2 jit_solution(15712786605914880732)
XLA Ops:
  0.0 71.4 %shard_map.91 = bf16[80,2048]{1,0:T(8,128)(2,1)} custom-call(s32[64]{0:T(128)} %tas.1, s32[5,16]{1,0:T(8,128)} %bitcast.1, s32[1,3]{1,0:T(1,128)} %plen.1, bf16[160,1024]{1,0:T(8,128)(2,1)} %q_hbm.1, bf16[160,128]{1,0:T(8,128)(2,1)} %k_hbm.1, bf16[160,128]{1,0:T(8,128)(2,1)} %v_hbm.1, bf16[1024,2048]{1,0:T(8,128)(2,1)} %w_hbm.1, bf16[4,64,256]{2,1,0:T(8,128)(2,1)} %dn_hbm.1, ...), custom_call_target="tpu_custom_call" | custom-call | tf_op jit(solution)/shard_map/pallas_call | solution.py:517
  71.4 1.7 %copy.11 = bf16[80,2048]{1,0:T(8,128)(2,1)} copy(bf16[80,2048]{1,0:T(8,128)(2,1)} %shard_map.91) | data formatting | bytes 655360

commit v6 on v5

--- a/solution.py
+++ b/solution.py
@@ -124,10 +124,11 @@
             zs.at[m, to], zr[m].at[z], zss.at[m, i - 1], zrs.at[m, i - 1], grp=y_lo * NZ + to
         )
 
-    for i in range(1, NZ):
-        @pl.when(z + i >= NZ)
-        def _():
-            z_copy(0, i).start()
+    for m in range(2):
+        for i in range(1, NZ):
+            @pl.when(z + i >= NZ)
+            def _():
+                z_copy(m, i).start()
 
     for m in range(2):
         for j in range(2):
@@ -206,10 +207,11 @@
     def _():
         pl.semaphore_wait(z_in, NZ - 1 - z)
 
-    for i in range(1, NZ):
-        @pl.when(z + i < NZ)
-        def _():
-            z_copy(0, i).start()
+    for m in range(2):
+        for i in range(1, NZ):
+            @pl.when(z + i < NZ)
+            def _():
+                z_copy(m, i).start()
 
     loads[5].wait()
 
@@ -388,8 +390,6 @@
     for side in range(2):
         later_copy(side, 1).start()
     x_phase(0)
-    for i in range(1, NZ):
-        z_copy(1, i).start()
     product(1)
     x_phase(1)
     cross_send(0)
@@ -401,6 +401,7 @@
     cross_take(0, down)
     for k in range(3):
         low_rank(k)
+    cross_send(1)
 
     for side in range(2):
         for piece in range(2):
@@ -426,7 +427,6 @@
     for i in range(1, NSP):
         ly_copy(i).start()
 
-    cross_send(1)
     cross_take(1, up2own)
     for i in range(1, NCHIP):
         up_copy(i).start()

time: 73.3 us -> 68.7 us (0.937)
  Pallas kernels: 71.4 us -> 66.8 us
    pallas_call x1, Pallas kernels: 71.4 us -> 66.8 us  [on_device(): pl.pallas_call(kernel, out_shape=jax.ShapeDtypeStruct((HALF, COLS), BF16)...]
where the time goes in v6:
time: 68.7 us; the launch traced here: 68.5 us
  Pallas kernels  66.8 us (97%)
  local copies, waits for them, and re-layouts  1.72 us (3%)
    pallas_call x1, Pallas kernels, on_device(): pl.pallas_call(kernel, out_shape=jax.ShapeDtypeStruct((HALF, COLS), BF16)...  66.8 us
    unnamed x1, local copies, waits for them, and re-layouts  1.72 us

profile of v6, /device:TPU:17, one launch (start us, length us, event | category | flops | bytes accessed | tf_op | source)
XLA Modules:
  0.0 68.5 jit_solution(17392585405056411901)
XLA Ops:
  0.0 66.8 %shard_map.91 = bf16[80,2048]{1,0:T(8,128)(2,1)} custom-call(s32[64]{0:T(128)} %tas.1, s32[5,16]{1,0:T(8,128)} %bitcast.1, s32[1,3]{1,0:T(1,128)} %plen.1, bf16[160,1024]{1,0:T(8,128)(2,1)} %q_hbm.1, bf16[160,128]{1,0:T(8,128)(2,1)} %k_hbm.1, bf16[160,128]{1,0:T(8,128)(2,1)} %v_hbm.1, bf16[1024,2048]{1,0:T(8,128)(2,1)} %w_hbm.1, bf16[4,64,256]{2,1,0:T(8,128)(2,1)} %dn_hbm.1, ...), custom_call_target="tpu_custom_call" | custom-call | tf_op jit(solution)/shard_map/pallas_call | solution.py:517
  66.8 1.7 %copy.11 = bf16[80,2048]{1,0:T(8,128)(2,1)} copy(bf16[80,2048]{1,0:T(8,128)(2,1)} %shard_map.91) | data formatting | bytes 655360

commit v7 on v6

--- a/solution.py
+++ b/solution.py
@@ -124,7 +124,7 @@
             zs.at[m, to], zr[m].at[z], zss.at[m, i - 1], zrs.at[m, i - 1], grp=y_lo * NZ + to
         )
 
-    for m in range(2):
+    for m in (1, 0):
         for i in range(1, NZ):
             @pl.when(z + i >= NZ)
             def _():
@@ -207,7 +207,7 @@
     def _():
         pl.semaphore_wait(z_in, NZ - 1 - z)
 
-    for m in range(2):
+    for m in (1, 0):
         for i in range(1, NZ):
             @pl.when(z + i < NZ)
             def _():

time: 68.7 us -> 68 us (0.990)
  Pallas kernels: 66.8 us -> 66.1 us
where the time goes in v7:
time: 68 us; the launch traced here: 67.8 us
  Pallas kernels  66.1 us (97%)
  local copies, waits for them, and re-layouts  1.72 us (3%)
    pallas_call x1, Pallas kernels, on_device(): pl.pallas_call(kernel, out_shape=jax.ShapeDtypeStruct((HALF, COLS), BF16)...  66.1 us
    unnamed x1, local copies, waits for them, and re-layouts  1.72 us

profile of v7, /device:TPU:17, one launch (start us, length us, event | category | flops | bytes accessed | tf_op | source)
XLA Modules:
  0.0 67.8 jit_solution(364978146480250757)
XLA Ops:
  0.0 66.1 %shard_map.91 = bf16[80,2048]{1,0:T(8,128)(2,1)} custom-call(s32[64]{0:T(128)} %tas.1, s32[5,16]{1,0:T(8,128)} %bitcast.1, s32[1,3]{1,0:T(1,128)} %plen.1, bf16[160,1024]{1,0:T(8,128)(2,1)} %q_hbm.1, bf16[160,128]{1,0:T(8,128)(2,1)} %k_hbm.1, bf16[160,128]{1,0:T(8,128)(2,1)} %v_hbm.1, bf16[1024,2048]{1,0:T(8,128)(2,1)} %w_hbm.1, bf16[4,64,256]{2,1,0:T(8,128)(2,1)} %dn_hbm.1, ...), custom_call_target="tpu_custom_call" | custom-call | tf_op jit(solution)/shard_map/pallas_call | solution.py:517
  66.1 1.7 %copy.11 = bf16[80,2048]{1,0:T(8,128)(2,1)} copy(bf16[80,2048]{1,0:T(8,128)(2,1)} %shard_map.91) | data formatting | bytes 655360

commit v8 on v7

--- a/solution.py
+++ b/solution.py
@@ -26,7 +26,7 @@
 PCOLS = COLS // PARTS
 TILE = 256
 STACK = 8
-PIECES = ((0, 32), (32, 48))
+PIECES = ((0, 16), (16, 64))
 
 adapter_scale = 0.5
 big_negative = -1e30
@@ -412,6 +412,11 @@
         if part > 0:
             x_part(3, part - 1)
     x_part(3, PARTS - 1)
+    cross_take(1, up2own)
+    for i in range(1, NCHIP):
+        up_copy(i).start()
+    up2[tp] = up2own[pl.ds(chip, 2)]
+    up_share(0).start()
 
     for rel in range(NTP - 1):
         copy_to(lxs.at[0, 0], lxr.at[rel], lxss.at[0, 0], lxrs.at[rel], tp=sib).wait_recv()
@@ -427,11 +432,6 @@
     for i in range(1, NSP):
         ly_copy(i).start()
 
-    cross_take(1, up2own)
-    for i in range(1, NCHIP):
-        up_copy(i).start()
-    up2[tp] = up2own[pl.ds(chip, 2)]
-    up_share(0).start()
     for i in range(1, NCHIP):
         up_copy(i).wait_recv()
         up_share(i).start()

time: 68 us -> 68 us (level)
  no operation moved by 1% of the time
where the time goes in v8:
time: 68 us; the launch traced here: 67.8 us
  Pallas kernels  66.1 us (97%)
  local copies, waits for them, and re-layouts  1.72 us (3%)
    pallas_call x1, Pallas kernels, on_device(): pl.pallas_call(kernel, out_shape=jax.ShapeDtypeStruct((HALF, COLS), BF16)...  66.1 us
    unnamed x1, local copies, waits for them, and re-layouts  1.72 us

profile of v8, /device:TPU:17, one launch (start us, length us, event | category | flops | bytes accessed | tf_op | source)
XLA Modules:
  0.0 67.8 jit_solution(5685272647408293330)
XLA Ops:
  0.0 66.1 %shard_map.91 = bf16[80,2048]{1,0:T(8,128)(2,1)} custom-call(s32[64]{0:T(128)} %tas.1, s32[5,16]{1,0:T(8,128)} %bitcast.1, s32[1,3]{1,0:T(1,128)} %plen.1, bf16[160,1024]{1,0:T(8,128)(2,1)} %q_hbm.1, bf16[160,128]{1,0:T(8,128)(2,1)} %k_hbm.1, bf16[160,128]{1,0:T(8,128)(2,1)} %v_hbm.1, bf16[1024,2048]{1,0:T(8,128)(2,1)} %w_hbm.1, bf16[4,64,256]{2,1,0:T(8,128)(2,1)} %dn_hbm.1, ...), custom_call_target="tpu_custom_call" | custom-call | tf_op jit(solution)/shard_map/pallas_call | solution.py:517
  66.1 1.7 %copy.11 = bf16[80,2048]{1,0:T(8,128)(2,1)} copy(bf16[80,2048]{1,0:T(8,128)(2,1)} %shard_map.91) | data formatting | bytes 655360
